TPU v7x, 32 devices: a whole 2x2x4 slice. The times are simulated.
32 devices in a mesh: groups: 2 (over y), tm: 4 (over z), dp: 2 (over x), head: 2 (over core).
Axes of the slice: x: 2, y: 2, z: 4, core: 2. Of those that a mesh axis runs over, the one named last changes fastest.
Arguments:
- tokens: bfloat16 [4, 8, 256, 1024], P(('groups', 'dp'), 'tm'), parts along dimension 0, may hold values from -6 to 6
- counts: int32 [4, 8], P(('groups', 'dp'), 'tm'), parts along dimension 0, may hold values from 64 to 256, as said below
- positions: int32 [4, 8, 256], P(('groups', 'dp'), 'tm'), parts along dimension 0, may hold values from 0 to 255, as said below
- cotangent: bfloat16 [4, 8, 256, 1024], P(('groups', 'dp'), 'tm'), parts along dimension 0, may hold values from -6 to 6
- w_qkv: bfloat16 [3, 1024, 1024], P(None, 'dp', 'head'), may hold values from -8 to 8
- w_out: bfloat16 [1024, 1024], P('head', 'dp'), may hold values from -0.1875 to 0.1875
Outputs:
- block_out: bfloat16 [4, 8, 256, 1024], P(('groups', 'dp'), 'tm'), parts along dimension 0
- token_grad: bfloat16 [4, 8, 256, 1024], P(('groups', 'dp'), 'tm'), parts along dimension 0
- out_weight_grad: float32 [2048, 1024], P(('groups', 'head'), 'dp'), parts along dimension 0
There are 2 independent parts, one for each index of `groups`. A program takes and returns all parts, laid end to end along the dimension named above; an argument that names none is the same for every part. Nothing has to cross between parts.
Inputs may be any that keep to these rules, and one draw needn't show every extreme that they name: `counts`: frame 0 of every clip keeps all 256 positions; every other frame keeps between 64 and 192. Each frame's row is a permutation of 0 to 255: the kept positions in ascending order in the first counts slots, then the others in ascending order.
All inputs are finite; a program needn't handle non-finite values.
Results may differ from a plain program's by a relative error of at most 0.012.
The roundings to bfloat16 on the way count: a program that leaves them out, or rounds other values in their place, can miss the bound.
Values may be sent and summed in bfloat16 or wider, within the bound.
A program may use at most 64 MiB of HBM per device.

v0:
```python
import jax
import jax.numpy as jnp
from jax import lax
from jax.sharding import PartitionSpec as P

HD = 64


epsilon = 1e-06


def normalize(tok_grid):
    full = tok_grid.astype(jnp.float32)
    centered = full - jnp.mean(full, axis=-1, keepdims=True)
    inv_std = lax.rsqrt(jnp.mean(centered * centered, axis=-1, keepdims=True) + epsilon)
    return (centered * inv_std, inv_std)


def normalize_back(d_hidden, normal, inv_std):
    centered = d_hidden - jnp.mean(d_hidden, axis=-1, keepdims=True)
    return inv_std * (centered - normal * jnp.mean(d_hidden * normal, axis=-1, keepdims=True))


def attend_forward(hidden, key_mask, w_part, o_part):
    frame_count, site_count, model_width = hidden.shape
    head_count = w_part.shape[2] // HD
    scale = float(HD) ** (-0.5)
    projected = jnp.einsum(
        "fsd,cde->cfse", hidden, w_part, preferred_element_type=jnp.float32
    ).astype(jnp.bfloat16)
    shape_four = (frame_count, site_count, head_count, HD)
    queries = projected[0].reshape(shape_four)
    key_rows = projected[1].reshape(shape_four)
    value_rows = projected[2].reshape(shape_four)
    scores = (
        jnp.einsum("fshc,gshc->shfg", queries, key_rows, preferred_element_type=jnp.float32) * scale
    )
    allowed = jnp.transpose(key_mask)[:, None, None, :]
    scores = jnp.where(allowed, scores, -1e30)
    row_top = jnp.max(scores, axis=-1, keepdims=True)
    expo = jnp.exp(scores - row_top)
    attn_probs = expo / jnp.sum(expo, axis=-1, keepdims=True)
    prob_bf = attn_probs.astype(jnp.bfloat16)
    attended = jnp.einsum(
        "shfg,gshc->fshc", prob_bf, value_rows, preferred_element_type=jnp.float32
    )
    attended = attended.astype(jnp.bfloat16).reshape(frame_count, site_count, head_count * HD)
    partial_out = jnp.einsum("fse,ed->fsd", attended, o_part, preferred_element_type=jnp.float32)
    return (partial_out, (queries, key_rows, value_rows, attn_probs, prob_bf, attended))


def attend_backward(cot_grid, saved, w_part, o_part):
    queries, key_rows, value_rows, attn_probs, prob_bf, attended = saved
    frame_count, site_count, head_count, head_size = queries.shape
    scale = float(HD) ** (-0.5)
    d_attended = jnp.einsum(
        "fsd,ed->fse", cot_grid, o_part, preferred_element_type=jnp.float32
    ).astype(jnp.bfloat16)
    d_wout = jnp.einsum("fse,fsd->ed", attended, cot_grid, preferred_element_type=jnp.float32)
    d_heads = d_attended.reshape(queries.shape)
    d_probs = jnp.einsum("fshc,gshc->shfg", d_heads, value_rows, preferred_element_type=jnp.float32)
    d_values = jnp.einsum(
        "shfg,fshc->gshc", prob_bf, d_heads, preferred_element_type=jnp.float32
    ).astype(jnp.bfloat16)
    d_scores = (
        attn_probs * (d_probs - jnp.sum(d_probs * attn_probs, axis=-1, keepdims=True)) * scale
    )
    d_scores = d_scores.astype(jnp.bfloat16)
    d_queries = jnp.einsum(
        "shfg,gshc->fshc", d_scores, key_rows, preferred_element_type=jnp.float32
    ).astype(jnp.bfloat16)
    d_keys = jnp.einsum(
        "shfg,fshc->gshc", d_scores, queries, preferred_element_type=jnp.float32
    ).astype(jnp.bfloat16)
    stacked = jnp.stack([d_queries, d_keys, d_values]).reshape(
        3, frame_count, site_count, head_count * head_size
    )
    d_hidden = jnp.einsum("cfse,cde->fsd", stacked, w_part, preferred_element_type=jnp.float32)
    return (d_hidden, d_wout)


def on_device(tokens, counts, positions, cotangent, w_qkv, w_out):
    slot_count = tokens.shape[2]
    slot_ids = jnp.arange(slot_count, dtype=jnp.int32)
    selector = (positions[:, :, None, :] == slot_ids[None, None, :, None]) & (
        slot_ids[None, None, None, :] < counts[:, :, None, None]
    )
    selector = selector.astype(jnp.bfloat16)
    tok_grid = jnp.einsum(
        "bfpk,bfkd->bfpd", selector, tokens, preferred_element_type=jnp.float32
    ).astype(jnp.bfloat16)
    cot_grid = jnp.einsum(
        "bfpk,bfkd->bfpd", selector, cotangent, preferred_element_type=jnp.float32
    ).astype(jnp.bfloat16)
    keep_grid = jnp.sum(selector, axis=3)
    full_qkv, full_out = (
        lax.all_gather(w_qkv, "dp", axis=1, tiled=True),
        lax.all_gather(w_out, "dp", axis=1, tiled=True),
    )
    tok_pos, cot_pos, keep_pos = (
        lax.all_to_all(tok_grid, "tm", split_axis=2, concat_axis=1, tiled=True),
        lax.all_to_all(cot_grid, "tm", split_axis=2, concat_axis=1, tiled=True),
        lax.all_to_all(keep_grid, "tm", split_axis=2, concat_axis=1, tiled=True),
    )
    normal, inv_std = normalize(tok_pos[0])
    hidden = normal.astype(jnp.bfloat16)
    partial_out, saved = attend_forward(hidden, keep_pos[0] > 0.5, full_qkv, full_out)
    out_sum = lax.psum(partial_out.astype(jnp.bfloat16), "head").astype(jnp.float32)
    out_pos = (tok_pos[0].astype(jnp.float32) + out_sum).astype(jnp.bfloat16)
    d_part, d_wout_part = attend_backward(cot_pos[0], saved, full_qkv, full_out)
    d_hidden = lax.psum(d_part.astype(jnp.bfloat16), "head").astype(jnp.float32)
    grad_pos = (cot_pos[0].astype(jnp.float32) + normalize_back(d_hidden, normal, inv_std)).astype(
        jnp.bfloat16
    )
    out_grid, grad_grid = (
        lax.all_to_all(out_pos[None], "tm", split_axis=1, concat_axis=2, tiled=True),
        lax.all_to_all(grad_pos[None], "tm", split_axis=1, concat_axis=2, tiled=True),
    )
    block_out = jnp.einsum(
        "bfpk,bfpd->bfkd", selector, out_grid, preferred_element_type=jnp.float32
    ).astype(jnp.bfloat16)
    token_grad = jnp.einsum(
        "bfpk,bfpd->bfkd", selector, grad_grid, preferred_element_type=jnp.float32
    ).astype(jnp.bfloat16)
    clip_summed = lax.psum_scatter(
        d_wout_part.astype(jnp.bfloat16), "dp", scatter_dimension=1, tiled=True
    )
    weight_grad = lax.psum(clip_summed, "tm").astype(jnp.float32)
    return (block_out, token_grad, weight_grad)


def solution(mesh):
    placed = (
        P(("groups", "dp"), "tm", None, None),
        P(("groups", "dp"), "tm"),
        P(("groups", "dp"), "tm", None),
        P(("groups", "dp"), "tm", None, None),
        P(None, "dp", "head"),
        P("head", "dp"),
    )
    return jax.shard_map(
        on_device,
        mesh=mesh,
        in_specs=placed,
        out_specs=(
            P(("groups", "dp"), "tm", None, None),
            P(("groups", "dp"), "tm", None, None),
            P(("groups", "head"), "dp"),
        ),
        check_vma=False,
    )
```

profile of v0, /device:TPU:16, one launch (start us, length us, event | category | flops | bytes accessed | tf_op | source)
XLA Modules:
  0.0 287.7 jit_solution(4598696267521368626)
XLA Ops:
  9.7 5.2 %all-to-all-start.1 = ((bf16[1,2,256]{1,0,2:T(2,128)(2,1)}), bf16[1,2,256]{1,0,2:T(2,128)(2,1)S(1)}, u32[]{:S(2)}, u32[]{:S(2)}) async-start(bf16[1,2,256]{1,0,2:T(2,128)(2,1)} %copy.149), calls=%async_computation.1 | async-start | bytes 262144 | tf_op jit(solution)/shard_map/all_to_all | solution.py:103
  18.8 5.7 %all-to-all-start = ((bf16[1,2,256,1024]{3,1,0,2:T(2,128)(2,1)}), bf16[1,2,256,1024]{3,1,0,2:T(2,128)(2,1)S(1)}, u32[]{:S(2)}, u32[]{:S(2)}) async-start(bf16[1,2,256,1024]{3,1,0,2:T(2,128)(2,1)} %copy.147), calls=%async_computation | async-start | bytes 2097152 | tf_op jit(solution)/shard_map/all_to_all | solution.py:101
  28.7 17.0 %all-to-all-done = bf16[1,2,256,1024]{3,1,0,2:T(2,128)(2,1)S(1)} async-done(((bf16[1,2,256,1024]{3,1,0,2:T(2,128)(2,1)}), bf16[1,2,256,1024]{3,1,0,2:T(2,128)(2,1)S(1)}, u32[]{:S(2)}, u32[]{:S(2)}) %all-to-all-start) | async-done | bytes 1048608 | tf_op jit(solution)/shard_map/all_to_all | solution.py:101
  45.7 7.5 %all-to-all-start.3 = ((bf16[1,2,256,1024]{3,1,0,2:T(2,128)(2,1)}), bf16[1,2,256,1024]{3,1,0,2:T(2,128)(2,1)}, u32[]{:S(2)}, u32[]{:S(2)}) async-start(bf16[1,2,256,1024]{3,1,0,2:T(2,128)(2,1)} %copy.161), calls=%async_computation.3 | async-start | bytes 2097152 | tf_op jit(solution)/shard_map/all_to_all | solution.py:102
  57.3 17.9 %all-to-all-done.3 = bf16[1,2,256,1024]{3,1,0,2:T(2,128)(2,1)} async-done(((bf16[1,2,256,1024]{3,1,0,2:T(2,128)(2,1)}), bf16[1,2,256,1024]{3,1,0,2:T(2,128)(2,1)}, u32[]{:S(2)}, u32[]{:S(2)}) %all-to-all-start.3) | async-done | bytes 1048608 | tf_op jit(solution)/shard_map/all_to_all | solution.py:102
  77.6 3.1 %convolution_convert_fusion.9 = bf16[8,64,512]{2,1,0:T(8,128)(2,1)} fusion(bf16[8,64,1024]{2,1,0:T(8,128)(2,1)} %bitcast.125, bf16[512,1024]{1,0:T(8,128)(2,1)} %all-gather.5.cloned.1.call-done), kind=kOutput, calls=%fused_computation.54 | convolution fusion | flops 537133056 | bytes 2621440 | tf_op jit(solution)/shard_map/fsd,ed->fse/dot_general | solution.py:56
  87.7 7.9 %all-gather.3.cloned.1.call-done = bf16[3,1024,512]{2,1,0:T(8,128)(2,1)} async-done(((bf16[3,512,512]{2,1,0:T(8,128)(2,1)}), bf16[3,1024,512]{2,1,0:T(8,128)(2,1)}) %all-gather.3.cloned.1.call-update) | async-done | bytes 3145744 | tf_op jit(solution)/shard_map/all_gather | solution.py:97
  95.6 4.4 %fusion.28 = bf16[3,8,64,512]{3,2,0,1:T(8,128)(2,1)S(1)} fusion(bf16[3,1024,512]{2,1,0:T(8,128)(2,1)} %all-gather.3.cloned.1.call-done, f32[8,64,1024]{2,1,0:T(8,128)} %bitcast_subtract_fusion, f32[8,64]{1,0:T(8,128)S(1)} %bitcast.141), kind=kOutput, calls=%fused_computation.36 | convolution fusion | flops 1612447744 | bytes 6817792 | tf_op jit(solution)/shard_map/fsd,cde->cfse/dot_general | solution.py:28
  108.3 4.2 %fusion.55 = f32[64,8,8,8]{2,3,1,0:T(8,128)} fusion(bf16[8,64,8,64]{3,2,1,0:T(8,128)(2,1)} %reshape.149, bf16[8,64,8,64]{3,2,1,0:T(8,128)(2,1)} %reshape_squeeze.9), kind=kOutput, calls=%fused_computation.67 | convolution fusion | flops 4194304 | bytes 1179648 | tf_op jit(solution)/shard_map/fshc,gshc->shfg/dot_general | solution.py:61
  112.5 5.1 %fusion.90 = (f32[64,8,8]{2,1,0:T(8,128)S(1)}, f32[64,8,8,8]{2,3,1,0:T(8,128)}) fusion(pred[64,8]{1,0:T(8,128)(4,1)S(1)} %copy.152, bf16[8,64,8,64]{3,2,1,0:T(8,128)(2,1)} %reshape_squeeze.11, bf16[8,64,8,64]{3,2,1,0:T(8,128)(2,1)} %reshape_squeeze.10), kind=kOutput, calls=%fused_computation.106 | convolution fusion | flops 4325383 | bytes 1196544 | tf_op jit(solution)/shard_map/sub | solution.py:41
  117.6 6.4 %fusion.35 = bf16[8,64,8,64]{3,0,2,1:T(8,128)(2,1)} fusion(f32[64,8,8,8]{2,3,1,0:T(8,128)} %fusion.55, bf16[8,64,8,64]{3,2,1,0:T(8,128)(2,1)} %reshape_squeeze.11, f32[64,8,8,8]{2,3,1,0:T(8,128)} %get-tuple-element.11, f32[64,8,8]{2,1,0:T(8,128)S(1)} %get-tuple-element.10), kind=kOutput, calls=%fused_computation.50 | convolution fusion | flops 4689927 | bytes 1327104 | tf_op jit(solution)/shard_map/shfg,gshc->fshc/dot_general | solution.py:69
  124.0 6.3 %fusion.36 = bf16[8,64,8,64]{3,0,2,1:T(8,128)(2,1)} fusion(f32[64,8,8,8]{2,3,1,0:T(8,128)} %fusion.55, bf16[8,64,8,64]{3,2,1,0:T(8,128)(2,1)} %reshape_squeeze.10, f32[64,8,8,8]{2,3,1,0:T(8,128)} %get-tuple-element.11, f32[64,8,8]{2,1,0:T(8,128)S(1)} %get-tuple-element.10), kind=kOutput, calls=%fused_computation.51 | convolution fusion | flops 4689927 | bytes 1327104 | tf_op jit(solution)/shard_map/shfg,fshc->gshc/dot_general | solution.py:72
  130.3 4.0 %fusion.37 = bf16[8,64,8,64]{3,0,2,1:T(8,128)(2,1)} fusion(bf16[8,64,8,64]{3,2,1,0:T(8,128)(2,1)} %reshape.149, f32[64,8,8,8]{2,3,1,0:T(8,128)} %get-tuple-element.11, f32[64,8,8]{2,1,0:T(8,128)S(1)} %get-tuple-element.10), kind=kOutput, calls=%fused_computation.52 | convolution fusion | flops 4521984 | bytes 1196032 | tf_op jit(solution)/shard_map/shfg,fshc->gshc/dot_general | solution.py:62
  152.2 2.6 stack.14
  154.7 3.2 %convolution_convert_fusion.8 = bf16[8,64,1024]{2,1,0:T(8,128)(2,1)} fusion(bf16[8,64,512]{2,1,0:T(8,128)(2,1)} %reshape.146, bf16[512,1024]{1,0:T(8,128)(2,1)} %all-gather.5.cloned.1.call-done), kind=kOutput, calls=%fused_computation.45 | convolution fusion | flops 537395200 | bytes 2621440 | tf_op jit(solution)/shard_map/fse,ed->fsd/dot_general | solution.py:48
  157.9 4.7 %bitcast_convert_fusion.1 = bf16[8,64,1024]{2,1,0:T(8,128)(2,1)} fusion(bf16[3,1024,512]{2,1,0:T(8,128)(2,1)} %all-gather.3.cloned.1.call-done, bf16[1,8,64,512]{3,2,0,1:T(8,128)(2,1)S(1)} %bitcast.133, bf16[1,8,64,512]{3,2,0,1:T(8,128)(2,1)S(1)} %bitcast.131, bf16[1,8,64,512]{3,2,0,1:T(8,128)(2,1)S(1)} %bitcast.132), kind=kOutput, calls=%fused_computation.15 | convolution fusion | flops 1612709888 | bytes 5767168 | tf_op jit(solution)/shard_map/cfse,cde->fsd/dot_general | solution.py:78
  162.6 21.7 %all-reduce.6.cloned.1.call-done = (bf16[8,64,1024]{2,1,0:T(8,128)(2,1)}, bf16[8,64,1024]{2,1,0:T(8,128)(2,1)}) async-done(((bf16[8,64,1024]{2,1,0:T(8,128)(2,1)}, bf16[8,64,1024]{2,1,0:T(8,128)(2,1)}), (bf16[8,64,1024]{2,1,0:T(8,128)(2,1)}, bf16[8,64,1024]{2,1,0:T(8,128)(2,1)})) %all-reduce.6.cloned.1.call-update) | async-done | bytes 2097168 | tf_op jit(solution)/shard_map/psum | solution.py:108
  184.4 2.7 convert_reduce_fusion
  188.8 5.1 %all-to-all-start.4 = ((bf16[1,8,64,1024]{3,2,0,1:T(8,128)(2,1)}), bf16[1,8,64,1024]{3,2,0,1:T(8,128)(2,1)}, u32[]{:S(2)}, u32[]{:S(2)}) async-start(bf16[1,8,64,1024]{3,2,0,1:T(8,128)(2,1)} %fusion.41), calls=%async_computation.4 | async-start | bytes 2097152 | tf_op jit(solution)/shard_map/all_to_all | solution.py:117
  193.9 3.1 %bitcast_convert_fusion = bf16[512,1024]{1,0:T(8,128)(2,1)} fusion(bf16[8,64,512]{2,1,0:T(8,128)(2,1)} %reshape.146, bf16[8,64,1024]{2,1,0:T(8,128)(2,1)} %bitcast.126), kind=kOutput, calls=%fused_computation.14 | convolution fusion | flops 537395200 | bytes 2621440 | tf_op jit(solution)/shard_map/fse,fsd->ed/dot_general | solution.py:59
  197.0 2.7 fusion.11
  199.7 17.1 %all-to-all-done.4 = bf16[1,8,64,1024]{3,2,0,1:T(8,128)(2,1)} async-done(((bf16[1,8,64,1024]{3,2,0,1:T(8,128)(2,1)}), bf16[1,8,64,1024]{3,2,0,1:T(8,128)(2,1)}, u32[]{:S(2)}, u32[]{:S(2)}) %all-to-all-start.4) | async-done | bytes 1048608 | tf_op jit(solution)/shard_map/all_to_all | solution.py:117
  216.8 6.9 %all-to-all-start.2 = ((bf16[1,8,64,1024]{3,2,0,1:T(8,128)(2,1)}), bf16[1,8,64,1024]{3,2,0,1:T(8,128)(2,1)S(1)}, u32[]{:S(2)}, u32[]{:S(2)}) async-start(bf16[1,8,64,1024]{3,2,0,1:T(8,128)(2,1)} %bitcast.130), calls=%async_computation.2 | async-start | bytes 2097152 | tf_op jit(solution)/shard_map/all_to_all | solution.py:116
  224.3 50.4 %all-reduce.4.cloned.1.call-done = bf16[512,512]{1,0:T(8,128)(2,1)} async-done(((bf16[512,512]{1,0:T(8,128)(2,1)}), bf16[512,512]{1,0:T(8,128)(2,1)}) %all-reduce.4.cloned.1.call-update) | async-done | bytes 524304 | tf_op jit(solution)/shard_map/psum | solution.py:128
  (83 shorter events, 59.0 us)
Async XLA Ops:
  7.2 7.7 %copy-start = (bf16[1,2,256,1024]{3,2,1,0:T(8,128)(2,1)S(1)}, bf16[1,2,256,1024]{3,2,1,0:T(8,128)(2,1)}, u32[]{:S(2)}) copy-start(bf16[1,2,256,1024]{3,2,1,0:T(8,128)(2,1)} %param.6) | copy-start | bytes 3145732
  9.7 9.1 %all-to-all-start.1 = ((bf16[1,2,256]{1,0,2:T(2,128)(2,1)}), bf16[1,2,256]{1,0,2:T(2,128)(2,1)S(1)}, u32[]{:S(2)}, u32[]{:S(2)}) async-start(bf16[1,2,256]{1,0,2:T(2,128)(2,1)} %copy.149), calls=%async_computation.1 | async-start | bytes 262144 | tf_op jit(solution)/shard_map/all_to_all | solution.py:103
  18.3 7.6 %copy-start.7 = (bf16[1,2,256,1024]{3,2,1,0:T(8,128)(2,1)S(1)}, bf16[1,2,256,1024]{3,2,1,0:T(8,128)(2,1)}, u32[]{:S(2)}) copy-start(bf16[1,2,256,1024]{3,2,1,0:T(8,128)(2,1)} %param.9) | copy-start | bytes 3145732
  18.3 7.6 %copy-start.12 = (s32[1,2,256]{2,1,0:T(2,128)S(1)}, s32[1,2,256]{2,1,0:T(2,128)}, u32[]{:S(2)}) copy-start(s32[1,2,256]{2,1,0:T(2,128)} %param.8) | copy-start | bytes 6148
  18.8 26.9 %all-to-all-start = ((bf16[1,2,256,1024]{3,1,0,2:T(2,128)(2,1)}), bf16[1,2,256,1024]{3,1,0,2:T(2,128)(2,1)S(1)}, u32[]{:S(2)}, u32[]{:S(2)}) async-start(bf16[1,2,256,1024]{3,1,0,2:T(2,128)(2,1)} %copy.147), calls=%async_computation | async-start | bytes 2097152 | tf_op jit(solution)/shard_map/all_to_all | solution.py:101
  24.5 53.2 %all-gather.5.cloned.1.call-start = ((), (), s32[]{:S(2)}) async-start(), calls=%async_computation.7 | async-start | bytes 1572864 | tf_op jit(solution)/shard_map/all_gather | solution.py:98
  25.2 70.4 %all-gather.3.cloned.1.call-start = ((), (), s32[]{:S(2)}) async-start(), calls=%async_computation.6 | async-start | bytes 4718592 | tf_op jit(solution)/shard_map/all_gather | solution.py:97
  45.7 7.8 %copy-start.2 = (bf16[1,2,256,1024]{3,1,0,2:T(2,128)(2,1)}, bf16[1,2,256,1024]{3,1,0,2:T(2,128)(2,1)S(1)}, u32[]{:S(2)}) copy-start(bf16[1,2,256,1024]{3,1,0,2:T(2,128)(2,1)S(1)} %all-to-all-done) | copy-start | bytes 3145732
  45.7 29.4 %all-to-all-start.3 = ((bf16[1,2,256,1024]{3,1,0,2:T(2,128)(2,1)}), bf16[1,2,256,1024]{3,1,0,2:T(2,128)(2,1)}, u32[]{:S(2)}, u32[]{:S(2)}) async-start(bf16[1,2,256,1024]{3,1,0,2:T(2,128)(2,1)} %copy.161), calls=%async_computation.3 | async-start | bytes 2097152 | tf_op jit(solution)/shard_map/all_to_all | solution.py:102
  53.2 131.2 %all-reduce.6.cloned.1.call-start = ((), (), s32[]{:S(2)}) async-start(), calls=%async_computation.10 | async-start | bytes 4194304 | tf_op jit(solution)/shard_map/psum | solution.py:108
  53.6 1.7 copy-start.3
  83.1 2.4 copy-start.1
  130.3 4.0 %copy-start.6 = (bf16[8,64,8,64]{3,2,1,0:T(8,128)(2,1)S(1)}, bf16[8,64,8,64]{3,2,1,0:T(8,128)(2,1)}, u32[]{:S(2)}) copy-start(bf16[8,64,8,64]{3,2,1,0:T(8,128)(2,1)} %reshape_squeeze.9) | copy-start | bytes 1572868
  130.3 4.0 %copy-start.13 = (f32[64,8,8,8]{2,3,1,0:T(8,128)S(1)}, f32[64,8,8,8]{2,3,1,0:T(8,128)}, u32[]{:S(2)}) copy-start(f32[64,8,8,8]{2,3,1,0:T(8,128)} %get-tuple-element.11) | copy-start | bytes 393220
  134.4 2.0 copy-start.8
  154.7 3.2 %copy-start.9 = (bf16[1,8,64,512]{3,2,1,0:T(8,128)(2,1)S(1)}, bf16[1,8,64,512]{3,2,1,0:T(8,128)(2,1)}, u32[]{:S(2)}) copy-start(bf16[1,8,64,512]{3,2,1,0:T(8,128)(2,1)} %stack.13) | copy-start | bytes 1572868
  154.7 3.2 %copy-start.10 = (bf16[1,8,64,512]{3,2,1,0:T(8,128)(2,1)S(1)}, bf16[1,8,64,512]{3,2,1,0:T(8,128)(2,1)}, u32[]{:S(2)}) copy-start(bf16[1,8,64,512]{3,2,1,0:T(8,128)(2,1)} %stack.12) | copy-start | bytes 1572868
  154.7 3.2 %copy-start.11 = (bf16[1,8,64,512]{3,2,1,0:T(8,128)(2,1)S(1)}, bf16[1,8,64,512]{3,2,1,0:T(8,128)(2,1)}, u32[]{:S(2)}) copy-start(bf16[1,8,64,512]{3,2,1,0:T(8,128)(2,1)} %stack.14) | copy-start | bytes 1572868
  184.4 2.7 copy-start.4
  184.4 2.7 copy-start.5
  188.8 28.0 %all-to-all-start.4 = ((bf16[1,8,64,1024]{3,2,0,1:T(8,128)(2,1)}), bf16[1,8,64,1024]{3,2,0,1:T(8,128)(2,1)}, u32[]{:S(2)}, u32[]{:S(2)}) async-start(bf16[1,8,64,1024]{3,2,0,1:T(8,128)(2,1)} %fusion.41), calls=%async_computation.4 | async-start | bytes 2097152 | tf_op jit(solution)/shard_map/all_to_all | solution.py:117
  193.9 29.8 %reduce-scatter.2.cloned.1.call-start = ((), (), s32[]{:S(2)}) async-start(), calls=%async_computation.8 | async-start | bytes 1572864 | tf_op jit(solution)/shard_map/reduce_scatter | solution.py:125
  216.8 62.8 %all-to-all-start.2 = ((bf16[1,8,64,1024]{3,2,0,1:T(8,128)(2,1)}), bf16[1,8,64,1024]{3,2,0,1:T(8,128)(2,1)S(1)}, u32[]{:S(2)}, u32[]{:S(2)}) async-start(bf16[1,8,64,1024]{3,2,0,1:T(8,128)(2,1)} %bitcast.130), calls=%async_computation.2 | async-start | bytes 2097152 | tf_op jit(solution)/shard_map/all_to_all | solution.py:116
  223.7 51.0 %all-reduce.4.cloned.1.call-start = ((), (), s32[]{:S(2)}) async-start(), calls=%async_computation.9 | async-start | bytes 1048576 | tf_op jit(solution)/shard_map/psum | solution.py:128
Sparse Core Ops, SparseCore 0:
  26.8 22.2 all-gather.4
  50.7 44.9 all-gather.2
  162.8 21.5 all-reduce.5
  197.3 21.1 reduce-scatter.1
  226.6 48.1 all-reduce.3
where the time goes:
time: 291 us; the launch traced here: 288 us
  waiting for transfers between devices  135 us (46%)
  matrix products  51.4 us (18%)
  local copies, waits for them, and re-layouts  39.8 us (14%)
  starting transfers between devices  30.4 us (10%)
  other arithmetic  17.7 us (6%)
  between operations  13.9 us (5%)
    psum x1, waiting for transfers between devices, on_device(): weight_grad = lax.psum(clip_summed, 'tm').astype(jnp.float32)  50.4 us
    psum x1, waiting for transfers between devices, on_device(): lax.psum(partial_out.astype(jnp.bfloat16), 'head').astype(jnp.float32)  21.7 us
    all_to_all x1, waiting for transfers between devices, on_device(): lax.all_to_all(cot_grid, 'tm', split_axis=2, concat_axis=1, tiled=True)  17.9 us
    all_to_all x1, waiting for transfers between devices, on_device(): lax.all_to_all(grad_pos[None], 'tm', split_axis=1, concat_axis=2, tiled=T...  17.1 us
    all_to_all x1, waiting for transfers between devices, on_device(): lax.all_to_all(tok_grid, 'tm', split_axis=2, concat_axis=1, tiled=True)  17 us
    all_gather x1, waiting for transfers between devices, on_device(): lax.all_gather(w_qkv, 'dp', axis=1, tiled=True)  7.88 us
    another operation x3, local copies, waits for them, and re-layouts, attend_backward(): jnp.stack([d_queries, d_keys, d_values])  7.65 us
    all_to_all x1, starting transfers between devices, on_device(): lax.all_to_all(cot_grid, 'tm', split_axis=2, concat_axis=1, tiled=True)  7.5 us
  transfers between devices with their start and end apart: 10, of which 7 were waited for; matrix products, arithmetic and copies ran while one was open for 12% of the time, Pallas kernels for 0%

commit v1 on v0

v1 whole, which is shorter than its diff:
```python
import functools

import jax
import jax.numpy as jnp
from jax import lax
from jax.experimental import pallas as pl
from jax.experimental.pallas import tpu as pltpu
from jax.sharding import PartitionSpec as P

HD = 64
PAIR = 2 * HD
EPS = 1e-06
BF = jnp.bfloat16
F32 = jnp.float32


def dot(a, b, ca, cb):
    return lax.dot_general(a, b, (((ca,), (cb,)), ((), ())), preferred_element_type=F32)


def remote(src, dst, sems, index, device):
    return pltpu.make_async_remote_copy(
        src_ref=src,
        dst_ref=dst,
        send_sem=sems[0].at[index],
        recv_sem=sems[1].at[index],
        device_id=device,
        device_id_type=pl.DeviceIdType.MESH,
    )


def kernel(
    dims, code_row, code_col, tok_ref, cot_ref, wqkv_ref, wout_ref,
    bo_ref, tg_ref, dw_ref,
    wbuf, obuf, tok_send, tok_grid, cot_send, cot_grid,
    normal_ref, inv_ref, hidden_ref, bias_ref, qkv, dqkv, att, datt, probs, wide,
    out_send, out_ret, grad_send, grad_ret,
    dw_own, dw_send, dw_recv, dwx_own, dwx_send, dwx_recv, dwz_send, dwz_recv, dwa,
    local_sem, wx0, wx1, wy0, wy1, wc0, wc1, cx0, cx1, cy0, cy1,
    zt0, zt1, zc0, zc1, zo0, zo1, zg0, zg1, ro0, ro1, rg0, rg1,
    dc0, dc1, dx0, dx1, ds0, ds1, da0, da1,
):
    T, X, G, H, FL, S, D, E, DL = dims
    rows = T * FL * S
    block = FL * S
    wx, wy, wc, cx, cy = (wx0, wx1), (wy0, wy1), (wc0, wc1), (cx0, cx1), (cy0, cy1)
    zt, zc, zo, zg = (zt0, zt1), (zc0, zc1), (zo0, zo1), (zg0, zg1)
    ro, rg, dc, dx, ds, da = (ro0, ro1), (rg0, rg1), (dc0, dc1), (dx0, dx1), (ds0, ds1), (da0, da1)
    g, z, x, h = (lax.axis_index(name) for name in ("groups", "tm", "dp", "head"))
    other_g, other_h = lax.rem(g + 1, G), lax.rem(h + 1, H)
    to_group, to_core = {"groups": other_g}, {"head": other_h}
    plus = lambda me, step, size: lax.rem(me + step, size)

    barrier = pltpu.get_barrier_semaphore()
    peers = [to_group, to_core]
    peers += [{"tm": plus(z, j, T)} for j in range(1, T)]
    peers += [{"dp": plus(x, j, X)} for j in range(1, X)]
    for peer in peers:
        pl.semaphore_signal(barrier, inc=1, device_id=peer, device_id_type=pl.DeviceIdType.MESH)
    pl.semaphore_wait(barrier, len(peers))

    pending = []

    def go(copy):
        copy.start()
        pending.append(copy)

    def w_in(i, half):
        if i < 3:
            return wqkv_ref.at[i, pl.ds(half * (DL // 2), DL // 2)]
        return wout_ref.at[pl.ds(half * (E // 2), E // 2)]

    def w_at(hh, xx, i, half):
        if i < 3:
            return wbuf.at[hh, xx, i, pl.ds(half * (DL // 2), DL // 2)]
        return obuf.at[hh, xx, pl.ds(half * (E // 2), E // 2)]

    def w_all(hh, xx, i):
        return wbuf.at[hh, xx, i] if i < 3 else obuf.at[hh, xx]

    for i in range(4):
        for j in range(1, X):
            go(remote(w_in(i, g), w_at(h, x, i, g), wx, (j - 1) * 4 + i, {"dp": plus(x, j, X)}))
    locals_ = []
    for i in range(4):
        mine = wqkv_ref.at[i] if i < 3 else wout_ref
        go(remote(mine, w_all(h, x, i), wc, i, to_core))
        copy = pltpu.make_async_copy(mine, w_all(h, x, i), local_sem.at[i])
        copy.start()
        locals_.append(copy)

    slots = code_row.shape[1]
    positions = slots // FL

    def row_code(shape, dim, core):
        r = lax.broadcasted_iota(jnp.int32, shape, dim)
        t = lax.div(r, block)
        f = lax.rem(lax.div(r, S), FL)
        s = lax.rem(r, S)
        return f * positions + (t * H + core) * S + s

    picked = row_code((rows, slots), 0, h) == code_row[...]
    chosen = jnp.where(picked, 1.0, 0.0)
    flags = jnp.sum(chosen, axis=1, keepdims=True)
    chosen = chosen.astype(BF)
    tok_send[:, :, :D] = dot(chosen, tok_ref[...], 1, 0).astype(BF).reshape(T, block, D)
    tok_send[:, :, D:] = jnp.broadcast_to(flags, (rows, 128)).astype(BF).reshape(T, block, 128)
    for j in range(1, T):
        t = plus(z, j, T)
        go(remote(tok_send.at[t], tok_grid.at[z], zt, j - 1, {"tm": t}))
    tok_grid[z] = tok_send[z]
    cot_send[...] = dot(chosen, cot_ref[...], 1, 0).astype(BF).reshape(T, block, D)
    for j in range(1, T):
        t = plus(z, j, T)
        go(remote(cot_send.at[t], cot_grid.at[z], zc, j - 1, {"tm": t}))
    cot_grid[z] = cot_send[z]

    def arrived(dst, sems, index, device):
        remote(dst, dst, sems, index, device).wait_recv()

    def forward_x(i):
        for j in range(1, X):
            src = plus(x, X - j, X)
            spot = w_at(h, src, i, g)
            arrived(spot, wx, (j - 1) * 4 + i, to_group)
            go(remote(spot, spot, wy, (j - 1) * 4 + i, to_group))
            go(remote(spot, spot, cx, (j - 1) * 4 + i, to_core))

    def forward_y(i):
        for j in range(1, X):
            src = plus(x, X - j, X)
            spot = w_at(h, src, i, other_g)
            arrived(spot, wy, (j - 1) * 4 + i, to_group)
            go(remote(spot, spot, cy, (j - 1) * 4 + i, to_core))

    def have_weights(i):
        locals_[i].wait()
        arrived(w_all(other_h, x, i), wc, i, to_core)
        for j in range(1, X):
            src = plus(x, X - j, X)
            arrived(w_at(other_h, src, i, g), cx, (j - 1) * 4 + i, to_core)
            arrived(w_at(other_h, src, i, other_g), cy, (j - 1) * 4 + i, to_core)

    forward_x(0)
    for j in range(1, T):
        arrived(tok_grid.at[plus(z, T - j, T)], zt, j - 1, to_core)

    full = tok_grid[:, :, :D].reshape(rows, D).astype(F32)
    centered = full - jnp.mean(full, axis=1, keepdims=True)
    inv_std = lax.rsqrt(jnp.mean(centered * centered, axis=1, keepdims=True) + EPS)
    normal = centered * inv_std
    normal_ref[...] = normal
    inv_ref[...] = jnp.broadcast_to(inv_std, inv_ref.shape)
    hidden_ref[...] = normal.astype(BF)
    first = jnp.where(lax.broadcasted_iota(jnp.int32, (16, 128), 1) == 0, 1.0, 0.0).astype(BF)
    keep = dot(first, tok_grid[:, :, D:].reshape(rows, 128), 1, 1)[0:1, :]
    ri = lax.broadcasted_iota(jnp.int32, (rows, rows), 0)
    ci = lax.broadcasted_iota(jnp.int32, (rows, rows), 1)
    allowed = (lax.rem(ri, S) == lax.rem(ci, S)) & (keep > 0.5)
    bias_ref[...] = jnp.where(allowed, 0.0, -1e30)

    def matmul_w(i, hh):
        total = jnp.zeros((rows, E), F32)
        for xx in range(X):
            total += dot(hidden_ref[:, xx * DL:(xx + 1) * DL], wbuf[hh, xx, i], 1, 0)
        return total.astype(BF)

    forward_x(1)
    forward_y(0)
    forward_x(2)
    have_weights(0)
    for hh in range(H):
        qkv[0, hh] = matmul_w(0, hh)
    forward_y(1)
    forward_x(3)
    have_weights(1)
    for hh in range(H):
        qkv[1, hh] = matmul_w(1, hh)
    forward_y(2)
    have_weights(2)
    for hh in range(H):
        qkv[2, hh] = matmul_w(2, hh)
    forward_y(3)

    pairs = E // PAIR
    scale = float(HD) ** (-0.5)
    lane = lax.broadcasted_iota(jnp.int32, (rows, PAIR), 1)
    left = lane < HD

    def half_of(value, second):
        keep_it = left if second == 0 else jnp.logical_not(left)
        return jnp.where(keep_it, value, jnp.zeros_like(value))

    def fwd(n, carry):
        hh, c = lax.div(n, pairs), lax.rem(n, pairs)
        cols = pl.ds(pl.multiple_of(c * PAIR, PAIR), PAIR)
        q, k, v = qkv[0, hh, :, cols], qkv[1, hh, :, cols], qkv[2, hh, :, cols]
        result = []
        for second in range(2):
            scores = dot(half_of(q, second), k, 1, 1) * scale + bias_ref[...]
            top = jnp.max(scores, axis=1, keepdims=True)
            expo = jnp.exp(scores - top)
            p = expo / jnp.sum(expo, axis=1, keepdims=True)
            probs[n, second] = p
            result.append(dot(p.astype(BF), v, 1, 0))
        att[hh, :, cols] = jnp.where(left, result[0], result[1]).astype(BF)
        return carry

    lax.fori_loop(0, H * pairs, fwd, 0)

    have_weights(3)
    for xx in range(X):
        total = jnp.zeros((rows, DL), F32)
        for hh in range(H):
            total += dot(att[hh], obuf[hh, xx], 1, 0).astype(BF).astype(F32)
        mine = tok_grid[:, :, xx * DL:(xx + 1) * DL].reshape(rows, DL).astype(F32)
        out_send[:, :, xx * DL:(xx + 1) * DL] = (mine + total).astype(BF).reshape(T, block, DL)
    for j in range(1, T):
        t = plus(z, j, T)
        go(remote(out_send.at[t], out_ret.at[h, z], zo, j - 1, {"tm": t}))
    out_ret[h, z] = out_send[z]
    go(remote(out_ret.at[h, z], out_ret.at[h, z], ro, 0, to_core))

    for j in range(1, T):
        arrived(cot_grid.at[plus(z, T - j, T)], zc, j - 1, to_core)

    def cot_cols(xx):
        return cot_grid[:, :, xx * DL:(xx + 1) * DL].reshape(rows, DL)

    for xx in range(X):
        dw_send[xx] = dot(att[other_h], cot_cols(xx), 0, 0).astype(BF)
    go(remote(dw_send, dw_recv, dc, 0, to_core))
    for xx in range(X):
        dw_own[xx] = dot(att[h], cot_cols(xx), 0, 0)

    for hh in range(H):
        total = jnp.zeros((rows, E), F32)
        for xx in range(X):
            total += dot(cot_cols(xx), obuf[hh, xx], 1, 1)
        datt[hh] = total.astype(BF)

    arrived(dw_recv, dc, 0, to_core)
    for j in range(1, X):
        to = plus(x, j, X)
        dwx_send[j - 1] = (dw_own[to] + dw_recv[to].astype(F32)).astype(BF)
        go(remote(dwx_send.at[j - 1], dwx_recv.at[j - 1], dx, j - 1, {"dp": to}))
    dwx_own[...] = dw_own[x] + dw_recv[x].astype(F32)

    def bwd(n, carry):
        hh, c = lax.div(n, pairs), lax.rem(n, pairs)
        cols = pl.ds(pl.multiple_of(c * PAIR, PAIR), PAIR)
        q, k, v = qkv[0, hh, :, cols], qkv[1, hh, :, cols], qkv[2, hh, :, cols]
        da_ = datt[hh, :, cols]
        dq, dk, dv = [], [], []
        for second in range(2):
            p = probs[n, second]
            dp_ = dot(half_of(da_, second), v, 1, 1)
            d_s = p * (dp_ - jnp.sum(dp_ * p, axis=1, keepdims=True)) * scale
            d_s = d_s.astype(BF)
            dv.append(dot(p.astype(BF), da_, 0, 0))
            dq.append(dot(d_s, k, 1, 0))
            dk.append(dot(d_s, q, 0, 0))
        dqkv[0, hh, :, cols] = jnp.where(left, dq[0], dq[1]).astype(BF)
        dqkv[1, hh, :, cols] = jnp.where(left, dk[0], dk[1]).astype(BF)
        dqkv[2, hh, :, cols] = jnp.where(left, dv[0], dv[1]).astype(BF)
        return carry

    lax.fori_loop(0, H * pairs, bwd, 0)

    for j in range(1, T):
        spot = out_ret.at[h, plus(z, T - j, T)]
        arrived(spot, zo, j - 1, to_core)
        go(remote(spot, spot, ro, j, to_core))

    for xx in range(X):
        total = jnp.zeros((rows, DL), F32)
        for hh in range(H):
            part = jnp.zeros((rows, DL), F32)
            for i in range(3):
                part += dot(dqkv[i, hh], wbuf[hh, xx, i], 1, 1)
            total += part.astype(BF).astype(F32)
        wide[:, xx * DL:(xx + 1) * DL] = total
    d_hidden = wide[...]
    normal = normal_ref[...]
    centered = d_hidden - jnp.mean(d_hidden, axis=1, keepdims=True)
    back = centered - normal * jnp.mean(d_hidden * normal, axis=1, keepdims=True)
    grad = cot_grid[...].reshape(rows, D).astype(F32) + inv_ref[:, 0:1] * back
    grad_send[...] = grad.astype(BF).reshape(T, block, D)
    for j in range(1, T):
        t = plus(z, j, T)
        go(remote(grad_send.at[t], grad_ret.at[h, z], zg, j - 1, {"tm": t}))
    grad_ret[h, z] = grad_send[z]
    go(remote(grad_ret.at[h, z], grad_ret.at[h, z], rg, 0, to_core))

    for j in range(1, X):
        arrived(dwx_recv.at[j - 1], dx, j - 1, to_core)
        dwx_own[...] += dwx_recv[j - 1].astype(F32)
    ET = E // T
    for j in range(1, T):
        t = plus(z, j, T)
        dwz_send[j - 1] = dwx_own[pl.ds(pl.multiple_of(t * ET, ET), ET), :].astype(BF)
        go(remote(dwz_send.at[j - 1], dwz_recv.at[j - 1], ds, j - 1, {"tm": t}))
    total = dwx_own[pl.ds(pl.multiple_of(z * ET, ET), ET), :]

    def back_code(shape, dim):
        r = lax.broadcasted_iota(jnp.int32, shape, dim)
        core = lax.div(r, rows)
        r = lax.rem(r, rows)
        t = lax.div(r, block)
        f = lax.rem(lax.div(r, S), FL)
        s = lax.rem(r, S)
        return f * positions + (t * H + core) * S + s

    unpick = jnp.where(code_col[...] == back_code((slots, H * rows), 1), 1.0, 0.0).astype(BF)
    for j in range(T):
        spot = out_ret.at[other_h, plus(z, T - j, T)]
        arrived(spot, ro, j, to_core)
    bo_ref[...] = dot(unpick, out_ret[...].reshape(H * rows, D), 1, 0).astype(BF)

    for j in range(1, T):
        arrived(dwz_recv.at[j - 1], ds, j - 1, to_core)
        total += dwz_recv[j - 1].astype(F32)
    dwa[z] = total.astype(BF)
    for j in range(1, T):
        go(remote(dwa.at[z], dwa.at[z], da, j - 1, {"tm": plus(z, j, T)}))

    for j in range(1, T):
        spot = grad_ret.at[h, plus(z, T - j, T)]
        arrived(spot, zg, j - 1, to_core)
        go(remote(spot, spot, rg, j, to_core))
    for j in range(T):
        arrived(grad_ret.at[other_h, plus(z, T - j, T)], rg, j, to_core)
    tg_ref[...] = dot(unpick, grad_ret[...].reshape(H * rows, D), 1, 0).astype(BF)
    for j in range(1, T):
        arrived(dwa.at[plus(z, T - j, T)], da, j - 1, to_core)
    dw_ref[...] = dwa[...].reshape(E, DL).astype(F32)
    for copy in pending:
        copy.wait_send()


def on_device(sizes, tokens, counts, positions, cotangent, w_qkv, w_out):
    G, T, X, H = sizes
    _, FL, slots, D = tokens.shape
    S = slots // (T * H)
    _, DL, E = w_qkv.shape
    rows, block = T * FL * S, FL * S
    frame = jnp.arange(FL, dtype=jnp.int32)[:, None] * slots
    kept = jnp.arange(slots, dtype=jnp.int32)[None, :] < counts[0][:, None]
    code = jnp.where(kept, positions[0] + frame, -1)
    dims = (T, X, G, H, FL, S, D, E, DL)
    pairs = E // PAIR
    vm = lambda *a: pltpu.VMEM(a[:-1], a[-1])
    sem = lambda n: [pltpu.SemaphoreType.DMA((n,))] * 2
    scratch = [
        vm(H, X, 3, DL, E, BF), vm(H, X, E, DL, BF),
        vm(T, block, D + 128, BF), vm(T, block, D + 128, BF), vm(T, block, D, BF), vm(T, block, D, BF),
        vm(rows, D, F32), vm(rows, 128, F32), vm(rows, D, BF), vm(rows, rows, F32),
        vm(3, H, rows, E, BF), vm(3, H, rows, E, BF), vm(H, rows, E, BF), vm(H, rows, E, BF),
        vm(H * pairs, 2, rows, rows, F32), vm(rows, D, F32),
        vm(T, block, D, BF), vm(H, T, block, D, BF), vm(T, block, D, BF), vm(H, T, block, D, BF),
        vm(X, E, DL, F32), vm(X, E, DL, BF), vm(X, E, DL, BF),
        vm(E, DL, F32), vm(X - 1, E, DL, BF), vm(X - 1, E, DL, BF),
        vm(T - 1, E // T, DL, BF), vm(T - 1, E // T, DL, BF), vm(T, E // T, DL, BF),
        pltpu.SemaphoreType.DMA((4,)),
    ]
    nx = 4 * (X - 1)
    for n in (nx, nx, 4, nx, nx, T - 1, T - 1, T - 1, T - 1, T, T, 1, X - 1, T - 1, T - 1):
        scratch += sem(n)
    in_vmem = pl.BlockSpec(memory_space=pltpu.VMEM)
    in_any = pl.BlockSpec(memory_space=pl.ANY)
    out, grad, dw = pl.pallas_call(
        functools.partial(kernel, dims),
        out_shape=(
            jax.ShapeDtypeStruct((FL * slots, D), BF),
            jax.ShapeDtypeStruct((FL * slots, D), BF),
            jax.ShapeDtypeStruct((E, DL), F32),
        ),
        in_specs=[in_vmem] * 4 + [in_any] * 2,
        out_specs=(in_vmem,) * 3,
        scratch_shapes=scratch,
        compiler_params=pltpu.CompilerParams(
            collective_id=0, has_side_effects=True, vmem_limit_bytes=58 * 1024 * 1024
        ),
    )(
        code.reshape(1, FL * slots), code.reshape(FL * slots, 1),
        tokens.reshape(FL * slots, D), cotangent.reshape(FL * slots, D), w_qkv, w_out,
    )
    return (out.reshape(tokens.shape), grad.reshape(tokens.shape), dw)


def solution(mesh):
    sizes = tuple(mesh.shape[name] for name in ("groups", "tm", "dp", "head"))
    placed = (
        P(("groups", "dp"), "tm", None, None),
        P(("groups", "dp"), "tm"),
        P(("groups", "dp"), "tm", None),
        P(("groups", "dp"), "tm", None, None),
        P(None, "dp", "head"),
        P("head", "dp"),
    )
    return jax.shard_map(
        functools.partial(on_device, sizes),
        mesh=mesh,
        in_specs=placed,
        out_specs=(
            P(("groups", "dp"), "tm", None, None),
            P(("groups", "dp"), "tm", None, None),
            P(("groups", "head"), "dp"),
        ),
        check_vma=False,
    )
```

time: 291 us -> 113 us (0.39); the launches traced: 288 us -> 113 us
  waiting for transfers between devices: 135 us -> 0 us
  Pallas kernels: 0 us -> 104 us
  matrix products: 51.4 us -> 0 us
  local copies, waits for them, and re-layouts: 39.8 us -> 5.61 us
  starting transfers between devices: 30.4 us -> 0 us
  other arithmetic: 17.7 us -> 2.06 us
  between operations: 13.9 us -> 0.69 us
    pallas_call x0 -> x1, Pallas kernels: none -> 104 us  [on_device(): pl.pallas_call(functools.partial(kernel, dims), out_shape=(jax.ShapeDtype...]
    psum x2 -> x0, waiting for transfers between devices: 72.2 us -> none  [the longest x1 50.4 us: on_device(): weight_grad = lax.psum(clip_summed, 'tm').astype(jnp.float32)]
    all_to_all x5 -> x0, waiting for transfers between devices: 52.5 us -> none  [the longest x1 17.9 us: on_device(): lax.all_to_all(cot_grid, 'tm', split_axis=2, concat_axis=1, tiled=True)]
    dot_general x14 -> x0, matrix products: 46.3 us -> none  [the longest x1 6.42 us: attend_backward(): jnp.einsum('shfg,gshc->fshc', d_scores, key_rows, preferred_element_type=...]
    all_to_all x5 -> x0, starting transfers between devices: 30.3 us -> none  [the longest x1 7.5 us: on_device(): lax.all_to_all(cot_grid, 'tm', split_axis=2, concat_axis=1, tiled=True)]
    another operation x6 -> x0, local copies, waits for them, and re-layouts: 14.7 us -> none  [the longest x3 7.65 us: attend_backward(): jnp.stack([d_queries, d_keys, d_values])]
    convert_element_type x7 -> x0, local copies, waits for them, and re-layouts: 13.9 us -> none  [the longest x1 2.33 us: attend_backward(): d_queries = jnp.einsum('shfg,gshc->fshc', d_scores, key_rows, preferred_e...]
    all_gather x2 -> x0, waiting for transfers between devices: 7.88 us -> none  [the longest x1 7.88 us: on_device(): lax.all_gather(w_qkv, 'dp', axis=1, tiled=True)]
  transfers between devices with their start and end apart: 10 -> 0, of which waited for: 7 -> 0; matrix products, arithmetic and copies ran while one was open for 12% -> 0% of each run, Pallas kernels for 0% -> 0%
where the time goes in v1:
time: 113 us
  Pallas kernels  104 us (92%)
  local copies, waits for them, and re-layouts  5.61 us (5%)
  other arithmetic  2.06 us (2%)
    pallas_call x1, Pallas kernels, on_device(): pl.pallas_call(functools.partial(kernel, dims), out_shape=(jax.ShapeDtype...  104 us
    unnamed x14, local copies, waits for them, and re-layouts  5.61 us

profile of v1, /device:TPU:16, one launch (start us, length us, event | category | flops | bytes accessed | tf_op | source)
XLA Modules:
  0.0 112.8 jit_solution(7808475169840254577)
XLA Ops:
  0.6 0.7 compare_bitcast_fusion
  1.4 0.1 broadcast_bitcast_fusion
  1.5 0.7 copy.13
  2.1 0.6 add_select_fusion.code_row
  2.7 0.2 copy.16
  2.9 0.1 copy.20
  3.1 0.1 copy.18
  3.2 0.7 fusion.code_col
  4.0 104.4 %shard_map.85 = (bf16[512,1024]{1,0:T(8,128)(2,1)}, bf16[512,1024]{1,0:T(8,128)(2,1)}, f32[512,512]{1,0:T(8,128)}) custom-call(s32[1,512]{1,0:T(1,128)} %add_select_fusion.code_row, s32[512,1]{1,0:T(8,128)} %fusion.code_col, bf16[512,1024]{1,0:T(8,128)(2,1)} %bitcast.33, bf16[512,1024]{1,0:T(8,128)(2,1)} %bitcast.34, bf16[3,512,512]{2,1,0:T(8,128)(2,1)} %wqkv_ref.1, ...), custom_call_target="tpu_custom_call" | custom-call | tf_op jit(solution)/shard_map/pallas_call | solution.py:371
  108.4 0.0 copy-start.1
  108.4 0.0 copy-start
  108.4 2.4 %copy.24 = bf16[1,2,256,1024]{3,2,1,0:T(8,128)(2,1)} copy(bf16[1,2,256,1024]{3,2,1,0:T(8,128)(2,1)} %bitcast.32) | data formatting | bytes 2097152
  110.9 0.0 copy-done.1
  110.9 1.0 copy.25
  111.8 0.0 copy-done
  111.8 1.0 copy.26
  (3 shorter events, 0.0 us)
Async XLA Ops:
  108.4 2.4 %copy-start.1 = (bf16[512,1024]{1,0:T(8,128)(2,1)S(1)}, bf16[512,1024]{1,0:T(8,128)(2,1)}, u32[]{:S(2)}) copy-start(bf16[512,1024]{1,0:T(8,128)(2,1)} %get-tuple-element.7) | copy-start | bytes 3145732
  108.4 3.4 %copy-start = (f32[512,512]{1,0:T(8,128)S(1)}, f32[512,512]{1,0:T(8,128)}, u32[]{:S(2)}) copy-start(f32[512,512]{1,0:T(8,128)} %get-tuple-element.14) | copy-start | bytes 3145732

commit v2 on v1

--- a/solution.py
+++ b/solution.py
@@ -9,6 +9,7 @@
 
 HD = 64
 PAIR = 2 * HD
+PIECES = 2
 EPS = 1e-06
 BF = jnp.bfloat16
 F32 = jnp.float32
@@ -35,7 +36,7 @@
     wbuf, obuf, tok_send, tok_grid, cot_send, cot_grid,
     normal_ref, inv_ref, hidden_ref, bias_ref, qkv, dqkv, att, datt, probs, wide,
     out_send, out_ret, grad_send, grad_ret,
-    dw_own, dw_send, dw_recv, dwx_own, dwx_send, dwx_recv, dwz_send, dwz_recv, dwa,
+    dw_own, dw_send, dw_recv, dwx_send, dwx_recv, dwz_send, dwz_recv, dwa,
     local_sem, wx0, wx1, wy0, wy1, wc0, wc1, cx0, cx1, cy0, cy1,
     zt0, zt1, zc0, zc1, zo0, zo1, zg0, zg1, ro0, ro1, rg0, rg1,
     dc0, dc1, dx0, dx1, ds0, ds1, da0, da1,
@@ -65,22 +66,27 @@
         copy.start()
         pending.append(copy)
 
-    def w_in(i, half):
-        if i < 3:
-            return wqkv_ref.at[i, pl.ds(half * (DL // 2), DL // 2)]
-        return wout_ref.at[pl.ds(half * (E // 2), E // 2)]
-
-    def w_at(hh, xx, i, half):
-        if i < 3:
-            return wbuf.at[hh, xx, i, pl.ds(half * (DL // 2), DL // 2)]
-        return obuf.at[hh, xx, pl.ds(half * (E // 2), E // 2)]
+    def unit_rows(u, half):
+        size = (DL if u < 3 * PIECES else E) // (2 * PIECES)
+        return pl.ds(pl.multiple_of((half * PIECES + u % PIECES) * size, size), size)
+
+    def w_in(u, half):
+        if u < 3 * PIECES:
+            return wqkv_ref.at[u // PIECES, unit_rows(u, half)]
+        return wout_ref.at[unit_rows(u, half)]
+
+    def w_at(hh, xx, u, half):
+        if u < 3 * PIECES:
+            return wbuf.at[hh, xx, u // PIECES, unit_rows(u, half)]
+        return obuf.at[hh, xx, unit_rows(u, half)]
 
     def w_all(hh, xx, i):
         return wbuf.at[hh, xx, i] if i < 3 else obuf.at[hh, xx]
 
-    for i in range(4):
+    units = 4 * PIECES
+    for u in range(units):
         for j in range(1, X):
-            go(remote(w_in(i, g), w_at(h, x, i, g), wx, (j - 1) * 4 + i, {"dp": plus(x, j, X)}))
+            go(remote(w_in(u, g), w_at(h, x, u, g), wx, (j - 1) * units + u, {"dp": plus(x, j, X)}))
     locals_ = []
     for i in range(4):
         mine = wqkv_ref.at[i] if i < 3 else wout_ref
@@ -118,28 +124,29 @@
     def arrived(dst, sems, index, device):
         remote(dst, dst, sems, index, device).wait_recv()
 
-    def forward_x(i):
+    def forward_x(u):
         for j in range(1, X):
             src = plus(x, X - j, X)
-            spot = w_at(h, src, i, g)
-            arrived(spot, wx, (j - 1) * 4 + i, to_group)
-            go(remote(spot, spot, wy, (j - 1) * 4 + i, to_group))
-            go(remote(spot, spot, cx, (j - 1) * 4 + i, to_core))
-
-    def forward_y(i):
+            spot = w_at(h, src, u, g)
+            arrived(spot, wx, (j - 1) * units + u, to_group)
+            go(remote(spot, spot, wy, (j - 1) * units + u, to_group))
+            go(remote(spot, spot, cx, (j - 1) * units + u, to_core))
+
+    def forward_y(u):
         for j in range(1, X):
             src = plus(x, X - j, X)
-            spot = w_at(h, src, i, other_g)
-            arrived(spot, wy, (j - 1) * 4 + i, to_group)
-            go(remote(spot, spot, cy, (j - 1) * 4 + i, to_core))
+            spot = w_at(h, src, u, other_g)
+            arrived(spot, wy, (j - 1) * units + u, to_group)
+            go(remote(spot, spot, cy, (j - 1) * units + u, to_core))
 
     def have_weights(i):
         locals_[i].wait()
         arrived(w_all(other_h, x, i), wc, i, to_core)
-        for j in range(1, X):
-            src = plus(x, X - j, X)
-            arrived(w_at(other_h, src, i, g), cx, (j - 1) * 4 + i, to_core)
-            arrived(w_at(other_h, src, i, other_g), cy, (j - 1) * 4 + i, to_core)
+        for u in range(i * PIECES, (i + 1) * PIECES):
+            for j in range(1, X):
+                src = plus(x, X - j, X)
+                arrived(w_at(other_h, src, u, g), cx, (j - 1) * units + u, to_core)
+                arrived(w_at(other_h, src, u, other_g), cy, (j - 1) * units + u, to_core)
 
     forward_x(0)
     for j in range(1, T):
@@ -165,22 +172,16 @@
             total += dot(hidden_ref[:, xx * DL:(xx + 1) * DL], wbuf[hh, xx, i], 1, 0)
         return total.astype(BF)
 
-    forward_x(1)
-    forward_y(0)
-    forward_x(2)
-    have_weights(0)
-    for hh in range(H):
-        qkv[0, hh] = matmul_w(0, hh)
-    forward_y(1)
-    forward_x(3)
-    have_weights(1)
-    for hh in range(H):
-        qkv[1, hh] = matmul_w(1, hh)
-    forward_y(2)
-    have_weights(2)
-    for hh in range(H):
-        qkv[2, hh] = matmul_w(2, hh)
-    forward_y(3)
+    def project(i):
+        have_weights(i)
+        for hh in range(H):
+            qkv[i, hh] = matmul_w(i, hh)
+
+    for u in range(1, units):
+        forward_x(u)
+        forward_y(u - 1)
+        if u % PIECES == PIECES - 1 and u >= 2 * PIECES - 1:
+            project(u // PIECES - 1)
 
     pairs = E // PAIR
     scale = float(HD) ** (-0.5)
@@ -206,7 +207,21 @@
         att[hh, :, cols] = jnp.where(left, result[0], result[1]).astype(BF)
         return carry
 
-    lax.fori_loop(0, H * pairs, fwd, 0)
+    lax.fori_loop(0, 2, fwd, 0)
+    forward_y(units - 1)
+    lax.fori_loop(2, H * pairs, fwd, 0)
+
+    for j in range(1, T):
+        arrived(cot_grid.at[plus(z, T - j, T)], zc, j - 1, to_core)
+
+    def cot_cols(xx):
+        return cot_grid[:, :, xx * DL:(xx + 1) * DL].reshape(rows, DL)
+
+    for xx in range(X):
+        dw_send[xx] = dot(att[other_h], cot_cols(xx), 0, 0).astype(BF)
+    go(remote(dw_send, dw_recv, dc, 0, to_core))
+    for xx in range(X):
+        dw_own[xx] = dot(att[h], cot_cols(xx), 0, 0)
 
     have_weights(3)
     for xx in range(X):
@@ -221,30 +236,37 @@
     out_ret[h, z] = out_send[z]
     go(remote(out_ret.at[h, z], out_ret.at[h, z], ro, 0, to_core))
 
-    for j in range(1, T):
-        arrived(cot_grid.at[plus(z, T - j, T)], zc, j - 1, to_core)
-
-    def cot_cols(xx):
-        return cot_grid[:, :, xx * DL:(xx + 1) * DL].reshape(rows, DL)
-
-    for xx in range(X):
-        dw_send[xx] = dot(att[other_h], cot_cols(xx), 0, 0).astype(BF)
-    go(remote(dw_send, dw_recv, dc, 0, to_core))
-    for xx in range(X):
-        dw_own[xx] = dot(att[h], cot_cols(xx), 0, 0)
-
     for hh in range(H):
         total = jnp.zeros((rows, E), F32)
         for xx in range(X):
             total += dot(cot_cols(xx), obuf[hh, xx], 1, 1)
         datt[hh] = total.astype(BF)
 
+    ET = E // T
+
+    def chunk(t):
+        return pl.ds(pl.multiple_of(t * ET, ET), ET)
+
     arrived(dw_recv, dc, 0, to_core)
-    for j in range(1, X):
-        to = plus(x, j, X)
-        dwx_send[j - 1] = (dw_own[to] + dw_recv[to].astype(F32)).astype(BF)
-        go(remote(dwx_send.at[j - 1], dwx_recv.at[j - 1], dx, j - 1, {"dp": to}))
-    dwx_own[...] = dw_own[x] + dw_recv[x].astype(F32)
+    for k in range(1, T + 1):
+        c = plus(z, k, T)
+        for j in range(1, X):
+            to = plus(x, j, X)
+            both = dw_own[to, chunk(c), :] + dw_recv[to, chunk(c), :].astype(F32)
+            dwx_send[j - 1, c] = both.astype(BF)
+            go(remote(dwx_send.at[j - 1, c], dwx_recv.at[j - 1, c], dx, (j - 1) * T + k - 1, {"dp": to}))
+
+    def dp_sum(k):
+        c = plus(z, k, T)
+        total = dw_own[x, chunk(c), :] + dw_recv[x, chunk(c), :].astype(F32)
+        for j in range(1, X):
+            arrived(dwx_recv.at[j - 1, c], dx, (j - 1) * T + k - 1, to_core)
+            total += dwx_recv[j - 1, c].astype(F32)
+        return total
+
+    def send_chunk(k):
+        dwz_send[k - 1] = dp_sum(k).astype(BF)
+        go(remote(dwz_send.at[k - 1], dwz_recv.at[k - 1], ds, k - 1, {"tm": plus(z, k, T)}))
 
     def bwd(n, carry):
         hh, c = lax.div(n, pairs), lax.rem(n, pairs)
@@ -265,7 +287,11 @@
         dqkv[2, hh, :, cols] = jnp.where(left, dv[0], dv[1]).astype(BF)
         return carry
 
-    lax.fori_loop(0, H * pairs, bwd, 0)
+    parts = 4
+    for part in range(parts):
+        lax.fori_loop(part * H * pairs // parts, (part + 1) * H * pairs // parts, bwd, 0)
+        for k in range(part * (T - 1) // parts, (part + 1) * (T - 1) // parts):
+            send_chunk(k + 1)
 
     for j in range(1, T):
         spot = out_ret.at[h, plus(z, T - j, T)]
@@ -292,15 +318,13 @@
     grad_ret[h, z] = grad_send[z]
     go(remote(grad_ret.at[h, z], grad_ret.at[h, z], rg, 0, to_core))
 
-    for j in range(1, X):
-        arrived(dwx_recv.at[j - 1], dx, j - 1, to_core)
-        dwx_own[...] += dwx_recv[j - 1].astype(F32)
-    ET = E // T
-    for j in range(1, T):
-        t = plus(z, j, T)
-        dwz_send[j - 1] = dwx_own[pl.ds(pl.multiple_of(t * ET, ET), ET), :].astype(BF)
-        go(remote(dwz_send.at[j - 1], dwz_recv.at[j - 1], ds, j - 1, {"tm": t}))
-    total = dwx_own[pl.ds(pl.multiple_of(z * ET, ET), ET), :]
+    total = dp_sum(T)
+    for j in range(1, T):
+        arrived(dwz_recv.at[j - 1], ds, j - 1, to_core)
+        total += dwz_recv[j - 1].astype(F32)
+    dwa[z] = total.astype(BF)
+    for j in range(1, T):
+        go(remote(dwa.at[z], dwa.at[z], da, j - 1, {"tm": plus(z, j, T)}))
 
     def back_code(shape, dim):
         r = lax.broadcasted_iota(jnp.int32, shape, dim)
@@ -318,13 +342,6 @@
     bo_ref[...] = dot(unpick, out_ret[...].reshape(H * rows, D), 1, 0).astype(BF)
 
     for j in range(1, T):
-        arrived(dwz_recv.at[j - 1], ds, j - 1, to_core)
-        total += dwz_recv[j - 1].astype(F32)
-    dwa[z] = total.astype(BF)
-    for j in range(1, T):
-        go(remote(dwa.at[z], dwa.at[z], da, j - 1, {"tm": plus(z, j, T)}))
-
-    for j in range(1, T):
         spot = grad_ret.at[h, plus(z, T - j, T)]
         arrived(spot, zg, j - 1, to_core)
         go(remote(spot, spot, rg, j, to_core))
@@ -333,7 +350,7 @@
     tg_ref[...] = dot(unpick, grad_ret[...].reshape(H * rows, D), 1, 0).astype(BF)
     for j in range(1, T):
         arrived(dwa.at[plus(z, T - j, T)], da, j - 1, to_core)
-    dw_ref[...] = dwa[...].reshape(E, DL).astype(F32)
+    dw_ref[...] = dwa[...].reshape(E, DL)
     for copy in pending:
         copy.wait_send()
 
@@ -359,12 +376,12 @@
         vm(H * pairs, 2, rows, rows, F32), vm(rows, D, F32),
         vm(T, block, D, BF), vm(H, T, block, D, BF), vm(T, block, D, BF), vm(H, T, block, D, BF),
         vm(X, E, DL, F32), vm(X, E, DL, BF), vm(X, E, DL, BF),
-        vm(E, DL, F32), vm(X - 1, E, DL, BF), vm(X - 1, E, DL, BF),
+        vm(X - 1, T, E // T, DL, BF), vm(X - 1, T, E // T, DL, BF),
         vm(T - 1, E // T, DL, BF), vm(T - 1, E // T, DL, BF), vm(T, E // T, DL, BF),
         pltpu.SemaphoreType.DMA((4,)),
     ]
-    nx = 4 * (X - 1)
-    for n in (nx, nx, 4, nx, nx, T - 1, T - 1, T - 1, T - 1, T, T, 1, X - 1, T - 1, T - 1):
+    nx = 4 * PIECES * (X - 1)
+    for n in (nx, nx, 4, nx, nx, T - 1, T - 1, T - 1, T - 1, T, T, 1, (X - 1) * T, T - 1, T - 1):
         scratch += sem(n)
     in_vmem = pl.BlockSpec(memory_space=pltpu.VMEM)
     in_any = pl.BlockSpec(memory_space=pl.ANY)
@@ -373,7 +390,7 @@
         out_shape=(
             jax.ShapeDtypeStruct((FL * slots, D), BF),
             jax.ShapeDtypeStruct((FL * slots, D), BF),
-            jax.ShapeDtypeStruct((E, DL), F32),
+            jax.ShapeDtypeStruct((E, DL), BF),
         ),
         in_specs=[in_vmem] * 4 + [in_any] * 2,
         out_specs=(in_vmem,) * 3,
@@ -385,7 +402,7 @@
         code.reshape(1, FL * slots), code.reshape(FL * slots, 1),
         tokens.reshape(FL * slots, D), cotangent.reshape(FL * slots, D), w_qkv, w_out,
     )
-    return (out.reshape(tokens.shape), grad.reshape(tokens.shape), dw)
+    return (out.reshape(tokens.shape), grad.reshape(tokens.shape), dw.astype(F32))
 
 
 def solution(mesh):

time: 113 us -> 107 us (0.947); the launches traced: 113 us -> 105 us
  Pallas kernels: 104 us -> 97 us
  local copies, waits for them, and re-layouts: 5.61 us -> 3.2 us
  other arithmetic: 2.06 us -> 4.35 us
    pallas_call x1, Pallas kernels: 104 us -> 97 us  [on_device(): pl.pallas_call(functools.partial(kernel, dims), out_shape=(jax.ShapeDtype...]
    unnamed x14 -> x13, local copies, waits for them, and re-layouts: 5.61 us -> 3.2 us
    convert_element_type x0 -> x1, other arithmetic: none -> 2.29 us  [on_device(): dw.astype(F32)]
where the time goes in v2:
time: 107 us; the launch traced here: 105 us
  Pallas kernels  97 us (91%)
  other arithmetic  4.35 us (4%)
  local copies, waits for them, and re-layouts  3.2 us (3%)
    pallas_call x1, Pallas kernels, on_device(): pl.pallas_call(functools.partial(kernel, dims), out_shape=(jax.ShapeDtype...  97 us
    unnamed x13, local copies, waits for them, and re-layouts  3.2 us
    convert_element_type x1, other arithmetic, on_device(): dw.astype(F32)  2.29 us

profile of v2, /device:TPU:16, one launch (start us, length us, event | category | flops | bytes accessed | tf_op | source)
XLA Modules:
  0.0 105.2 jit_solution(3648434671648983654)
XLA Ops:
  0.6 0.7 compare_bitcast_fusion
  1.4 0.1 broadcast_bitcast_fusion
  1.5 0.7 copy.13
  2.1 0.6 add_select_fusion.code_row
  2.7 0.2 copy.16
  2.9 0.1 copy.20
  3.1 0.1 copy.18
  3.2 0.7 fusion.code_col
  4.0 97.0 %shard_map.85 = (bf16[512,1024]{1,0:T(8,128)(2,1)}, bf16[512,1024]{1,0:T(8,128)(2,1)}, bf16[512,512]{1,0:T(8,128)(2,1)}) custom-call(s32[1,512]{1,0:T(1,128)} %add_select_fusion.code_row, s32[512,1]{1,0:T(8,128)} %fusion.code_col, bf16[512,1024]{1,0:T(8,128)(2,1)} %bitcast.33, bf16[512,1024]{1,0:T(8,128)(2,1)} %bitcast.34, bf16[3,512,512]{2,1,0:T(8,128)(2,1)} %wqkv_ref.1, ...), custom_call_target="tpu_custom_call" | custom-call | tf_op jit(solution)/shard_map/pallas_call | solution.py:388
  101.0 0.0 copy-start.1
  101.0 0.0 copy-start
  101.0 2.3 %convert_element_type.3 = f32[512,512]{1,0:T(8,128)} convert(bf16[512,512]{1,0:T(8,128)(2,1)} %get-tuple-element.8) | non-fusion elementwise | flops 262144 | bytes 1572864 | tf_op jit(solution)/shard_map/convert_element_type | solution.py:405
  103.3 0.0 copy-done.1
  103.3 1.0 copy.23
  104.3 0.0 copy-done
  104.3 1.0 copy.24
  (3 shorter events, 0.0 us)
Async XLA Ops:
  101.0 2.3 %copy-start.1 = (bf16[512,1024]{1,0:T(8,128)(2,1)S(1)}, bf16[512,1024]{1,0:T(8,128)(2,1)}, u32[]{:S(2)}) copy-start(bf16[512,1024]{1,0:T(8,128)(2,1)} %get-tuple-element.6) | copy-start | bytes 3145732
  101.0 3.3 %copy-start = (bf16[512,1024]{1,0:T(8,128)(2,1)S(1)}, bf16[512,1024]{1,0:T(8,128)(2,1)}, u32[]{:S(2)}) copy-start(bf16[512,1024]{1,0:T(8,128)(2,1)} %get-tuple-element.7) | copy-start | bytes 3145732
